TPU v7x, 32 devices: a whole 2x2x4 slice. The times are simulated.
32 devices in a mesh: row: 8 (over y, x, core), col: 4 (over z).
Axes of the slice: x: 2, y: 2, z: 4, core: 2. Of those that a mesh axis runs over, the one named last changes fastest.
Arguments:
- density: bfloat16 [4096, 4096], P('row', 'col'), may hold values from -1.25 to 1.25, as said below
- hamiltonian: bfloat16 [4096, 4096], P('row', 'col'), may hold values from -60 to 60, as said below
- density_pattern: int32 [64, 64], replicated, may hold values from 0 to 1, as said below
- ham_pattern: int32 [64, 64], replicated, may hold values from 0 to 1, as said below
- source: int32 [64], replicated, may hold values from 0 to 63, as said below
Outputs:
- gradient: float32 [4096, 4096], P('row', 'col')
Inputs may be any that keep to these rules, and one draw needn't show every extreme that they name: density is symmetric. hamiltonian is symmetric. `density_pattern`: symmetric, with ones on the diagonal. `ham_pattern`: symmetric, with ones on the diagonal. `source`: a permutation; cut the positions into panels of 8 in order, the last panel and the first being neighbours too: every block either keeps its position or trades it with a block of a neighbouring panel, and from one panel to a neighbouring one at most 2 blocks move, exactly 2 for some pair of panels.
All inputs are finite; a program needn't handle non-finite values.
Results may differ from a plain program's by a relative error of at most 0.0025.
Values may be sent and summed in bfloat16 or wider, within the bound.
A program may use at most 128 MiB of HBM per device.

v0:
```python
import jax
import jax.numpy as jnp
from jax import lax
from jax.sharding import PartitionSpec as P

BLK = 64
CAP = 2


def shifted(block, axis, distance):
    devices = range(lax.axis_size(axis))
    route = [((i - distance) % len(devices), i) for i in devices]
    return lax.ppermute(block, axis, route)


def arrivals(source, target, extent, anchor):
    anchors = lax.dynamic_slice_in_dim(source, target * extent, extent)
    chosen = anchors // extent == anchor
    order_rank = jnp.cumsum(chosen.astype(jnp.int32)) - 1
    return (chosen, order_rank, anchors % extent)


def outgoing(blocks, source, target, anchor, extent, moving_axis):
    chosen, order_rank, within = arrivals(source, target, extent, anchor)
    places = jnp.arange(CAP, dtype=jnp.int32)
    matched = (order_rank[None, :] == places[:, None]) & chosen[None, :]
    picked = jnp.sum(jnp.where(matched, within[None, :], 0), axis=1)
    filled = jnp.any(matched, axis=1)
    selected = jnp.take(blocks, picked, axis=moving_axis)
    layout = [1] * blocks.ndim
    layout[moving_axis] = CAP
    return selected * filled.reshape(layout).astype(blocks.dtype)


def assemble(blocks, from_lower, from_upper, source, position, members, extent, moving_axis):
    anchors = lax.dynamic_slice_in_dim(source, position * extent, extent)
    home_panel = anchors // extent
    lower_hit = home_panel == (position - 1) % members
    upper_hit = home_panel == (position + 1) % members
    lower_rank = jnp.cumsum(lower_hit.astype(jnp.int32)) - 1
    upper_rank = jnp.cumsum(upper_hit.astype(jnp.int32)) - 1
    picked = jnp.where(
        lower_hit,
        extent + lower_rank,
        jnp.where(upper_hit, extent + CAP + upper_rank, anchors % extent),
    )
    stacked = jnp.concatenate((blocks, from_lower, from_upper), axis=moving_axis)
    return jnp.take(stacked, picked, axis=moving_axis)


def relocate_rows(local_tile, source):
    position = lax.axis_index("row")
    members = lax.axis_size("row")
    extent = local_tile.shape[0] // BLK
    blocks = local_tile.reshape(extent, BLK, local_tile.shape[1])
    upward = outgoing(blocks, source, (position + 1) % members, position, extent, 0)
    downward = outgoing(blocks, source, (position - 1) % members, position, extent, 0)
    from_lower = shifted(upward, "row", 1)
    from_upper = shifted(downward, "row", -1)
    placed = assemble(blocks, from_lower, from_upper, source, position, members, extent, 0)
    return placed.reshape(local_tile.shape)


def apply_pattern(matrix, pattern):
    rows_b = pattern.shape[0]
    cols_b = pattern.shape[1]
    blocks = matrix.reshape(rows_b, BLK, cols_b, BLK)
    return (blocks * pattern[:, None, :, None].astype(matrix.dtype)).reshape(matrix.shape)


def multiply(panel, operand):
    return jnp.dot(
        panel,
        lax.all_gather(operand, "row", axis=0, tiled=True),
        preferred_element_type=jnp.float32,
    )


def body(density, hamiltonian, density_pattern, ham_pattern, source):
    row_position = lax.axis_index("row")
    col_position = lax.axis_index("col")
    block_rows = density.shape[0] // BLK
    block_cols = density.shape[1] // BLK
    rows_done = relocate_rows(density, source)
    panel = lax.all_gather(rows_done, "col", axis=1, tiled=True)
    total_blocks = panel.shape[1] // BLK
    panel = jnp.take(panel.reshape(panel.shape[0], total_blocks, BLK), source, axis=1).reshape(
        panel.shape
    )
    row_pattern = lax.dynamic_slice_in_dim(
        density_pattern, row_position * block_rows, block_rows, 0
    )
    panel = apply_pattern(panel, row_pattern)
    tile_pattern = lax.dynamic_slice(
        ham_pattern,
        (row_position * block_rows, col_position * block_cols),
        (block_rows, block_cols),
    )
    ham_tile = apply_pattern(hamiltonian, tile_pattern)
    first = multiply(panel, ham_tile).astype(jnp.bfloat16)
    second = multiply(panel, first)
    return 3.0 * first.astype(jnp.float32) - 2.0 * second


def solution(mesh):
    return jax.shard_map(
        body,
        mesh=mesh,
        in_specs=(P("row", "col"), P("row", "col"), P(), P(), P()),
        out_specs=P("row", "col"),
        check_vma=False,
    )
```

profile of v0, /device:TPU:0, one launch (start us, length us, event | category | flops | bytes accessed | tf_op | source)
XLA Modules:
  0.0 243.6 jit_solution(12064904285664791367)
XLA Ops:
  6.5 0.7 fusion.3
  7.3 0.2 reduce-window.35
  7.5 0.2 reduce-window.34
  7.6 0.9 compare_and_fusion.4
  8.5 0.2 reduce-window.37
  8.7 0.1 select_reduce_fusion
  8.8 0.2 reduce-window.36
  9.0 0.1 fusion.1
  9.2 1.8 gather_fusion.3
  11.1 3.4 %collective-permute-start.1 = (bf16[2,64,1024]{2,1,0:T(8,128)(2,1)S(1)}, bf16[2,64,1024]{2,1,0:T(8,128)(2,1)S(1)}, u32[]{:S(2)}, u32[]{:S(2)}) collective-permute-start(bf16[2,64,1024]{2,1,0:T(8,128)(2,1)S(1)} %select_multiply_fusion), channel_id=1, source_target_pairs={{4,0},{8,4},{12,8},{16,12},{20,16},{24,20},{28,24},{0,28},{5,1},{9... | collective-permute-start | bytes 786440 | tf_op jit(solution)/shard_map/ppermute | solution.py:13
  14.6 1.8 gather_fusion.2
  16.8 3.2 %collective-permute-done.1 = bf16[2,64,1024]{2,1,0:T(8,128)(2,1)S(1)} collective-permute-done((bf16[2,64,1024]{2,1,0:T(8,128)(2,1)S(1)}, bf16[2,64,1024]{2,1,0:T(8,128)(2,1)S(1)}, u32[]{:S(2)}, u32[]{:S(2)}) %collective-permute-start.1) | collective-permute-done | bytes 262176 | tf_op jit(solution)/shard_map/ppermute | solution.py:13
  20.0 3.3 %collective-permute-done = bf16[2,64,1024]{2,1,0:T(8,128)(2,1)S(1)} collective-permute-done((bf16[2,64,1024]{2,1,0:T(8,128)(2,1)S(1)}, bf16[2,64,1024]{2,1,0:T(8,128)(2,1)S(1)}, u32[]{:S(2)}, u32[]{:S(2)}) %collective-permute-start) | collective-permute-done | bytes 262176 | tf_op jit(solution)/shard_map/ppermute | solution.py:13
  23.3 1.4 pad_maximum_fusion
  24.7 0.6 gather_fusion
  25.3 1.2 bitcast_select_fusion.1
  26.6 0.8 dynamic-slice_convert_fusion
  27.4 0.3 mul.75
  27.7 1.5 mul.76
  29.2 2.7 %mul.77 = bf16[512,1024]{1,0:T(8,128)(2,1)} multiply(bf16[512,1024]{1,0:T(8,128)(2,1)} %param.8, bf16[512,1024]{1,0:T(8,128)(2,1)S(1)} %mul.76) | non-fusion elementwise | flops 524288 | bytes 3145728 | tf_op jit(solution)/shard_map/mul | solution.py:68
  31.9 0.2 all-gather.8.cloned.1.call-start
  32.1 0.7 dynamic-slice_convert_fusion.1
  33.0 4.4 %mul.71 = bf16[8,64,64,64]{1,0,3,2:T(8,128)(2,1)} broadcast(bf16[8,64]{0,1:T(8,128)(2,1)S(1)} %copy.10), dimensions={0,2} | broadcast | bytes 4195328 | tf_op jit(solution)/shard_map/mul | solution.py:68
  37.3 11.8 %mul.72 = bf16[512,4096]{0,1:T(8,128)(2,1)} reshape(bf16[8,64,64,64]{1,0,3,2:T(8,128)(2,1)} %mul.71) | data formatting | bytes 8388608 | tf_op jit(solution)/shard_map/mul | solution.py:68
  49.4 57.5 %all-gather.4.cloned.1.call-done = bf16[512,4096]{1,0:T(8,128)(2,1)} async-done(((bf16[512,1024]{1,0:T(8,128)(2,1)}), bf16[512,4096]{1,0:T(8,128)(2,1)}) %all-gather.4.cloned.1.call-update) | async-done | bytes 4194320 | tf_op jit(solution)/shard_map/all_gather | solution.py:85
  106.8 6.5 %copy.9 = bf16[512,4096]{0,1:T(8,128)(2,1)} copy(bf16[512,4096]{1,0:T(8,128)(2,1)} %all-gather.4.cloned.1.call-done) | data formatting | bytes 8388608 | tf_op jit(solution)/shard_map/all_gather | solution.py:85
  113.3 5.5 %gather_fusion.1 = bf16[64,512,64]{1,2,0:T(8,128)(2,1)} fusion(bf16[512,64,64]{0,2,1:T(8,128)(2,1)} %bitcast.42, s32[1024]{0:T(1024)S(1)} %pad_clamp_fusion), kind=kCustom, calls=%fused_computation.3 | custom fusion | bytes 8388864 | tf_op jit(solution)/shard_map/jit(_take)/gather | solution.py:87
  118.8 5.2 %fusion = bf16[512,4096]{0,1:T(8,128)(2,1)} fusion(bf16[512,4096]{0,1:T(8,128)(2,1)} %mul.72, bf16[64,512,64]{1,2,0:T(8,128)(2,1)} %gather_fusion.1, pred[4096]{0:T(1024)(128)(4,1)S(1)} %broadcast_in_dim.70), kind=kLoop, calls=%fused_computation.5 | loop fusion | flops 4194304 | bytes 12587008 | tf_op jit(solution)/shard_map/mul | solution.py:68
  124.0 37.7 %all-gather.6.cloned.1.call-done = bf16[4096,1024]{1,0:T(8,128)(2,1)} async-done(((bf16[512,1024]{1,0:T(8,128)(2,1)}), bf16[4096,1024]{1,0:T(8,128)(2,1)}) %all-gather.6.cloned.1.call-update) | async-done | bytes 8388624 | tf_op jit(solution)/shard_map/all_gather | solution.py:74
  161.7 10.2 %convolution_convert_fusion = bf16[512,1024]{1,0:T(8,128)(2,1)} fusion(bf16[512,4096]{0,1:T(8,128)(2,1)} %fusion, bf16[4096,1024]{1,0:T(8,128)(2,1)} %all-gather.6.cloned.1.call-done), kind=kOutput, calls=%fused_computation.8 | convolution fusion | flops 4295491584 | bytes 13631488 | tf_op jit(solution)/shard_map/dot_general | solution.py:72
  171.9 54.5 %all-gather.8.cloned.1.call-done = bf16[4096,1024]{1,0:T(8,128)(2,1)} async-done(((bf16[512,1024]{1,0:T(8,128)(2,1)}), bf16[4096,1024]{1,0:T(8,128)(2,1)}) %all-gather.8.cloned.1.call-update) | async-done | bytes 8388624 | tf_op jit(solution)/shard_map/all_gather | solution.py:74
  226.5 10.6 %multiply_subtract_fusion = f32[512,1024]{1,0:T(8,128)} fusion(bf16[512,1024]{1,0:T(8,128)(2,1)} %convolution_convert_fusion, bf16[512,4096]{0,1:T(8,128)(2,1)} %fusion, bf16[4096,1024]{1,0:T(8,128)(2,1)} %all-gather.8.cloned.1.call-done), kind=kOutput, calls=%fused_computation.6 | convolution fusion | flops 4297064448 | bytes 15728640 | tf_op jit(solution)/shard_map/dot_general | solution.py:72
  (32 shorter events, 1.0 us)
Async XLA Ops:
  6.5 100.3 %all-gather.4.cloned.1.call-start = ((), (), s32[]{:S(2)}) async-start(), calls=%async_computation | async-start | bytes 5242880 | tf_op jit(solution)/shard_map/all_gather | solution.py:85
  11.1 8.9 %collective-permute-start.1 = (bf16[2,64,1024]{2,1,0:T(8,128)(2,1)S(1)}, bf16[2,64,1024]{2,1,0:T(8,128)(2,1)S(1)}, u32[]{:S(2)}, u32[]{:S(2)}) collective-permute-start(bf16[2,64,1024]{2,1,0:T(8,128)(2,1)S(1)} %select_multiply_fusion), channel_id=1, source_target_pairs={{4,0},{8,4},{12,8},{16,12},{20,16},{24,20},{28,24},{0,28},{5,1},{9... | collective-permute-start | bytes 786440 | tf_op jit(solution)/shard_map/ppermute | solution.py:13
  16.5 6.7 %collective-permute-start = (bf16[2,64,1024]{2,1,0:T(8,128)(2,1)S(1)}, bf16[2,64,1024]{2,1,0:T(8,128)(2,1)S(1)}, u32[]{:S(2)}, u32[]{:S(2)}) collective-permute-start(bf16[2,64,1024]{2,1,0:T(8,128)(2,1)S(1)} %select_multiply_fusion.1), channel_id=1, source_target_pairs={{28,0},{0,4},{4,8},{8,12},{12,16},{16,20},{20,24},{24,28},{29,1},{... | collective-permute-start | bytes 786440 | tf_op jit(solution)/shard_map/ppermute | solution.py:13
  26.5 135.1 %all-gather.6.cloned.1.call-start = ((), (), s32[]{:S(2)}) async-start(), calls=%async_computation.1 | async-start | bytes 9437184 | tf_op jit(solution)/shard_map/all_gather | solution.py:74
  31.9 194.5 %all-gather.8.cloned.1.call-start = ((), (), s32[]{:S(2)}) async-start(), calls=%async_computation.2 | async-start | bytes 9437184 | tf_op jit(solution)/shard_map/all_gather | solution.py:74
  37.3 11.8 %copy-start = (s32[64]{0:T(128)S(1)}, s32[64]{0:T(128)}, u32[]{:S(2)}) copy-start(s32[64]{0:T(128)} %param.11) | copy-start | bytes 772
Sparse Core Ops, SparseCore 0:
  26.7 80.1 all-gather.3
  108.7 52.9 all-gather.5
  172.0 54.3 all-gather.7
where the time goes:
time: 244 us
  waiting for transfers between devices  156 us (64%)
  local copies, waits for them, and re-layouts  34.6 us (14%)
  matrix products  20.9 us (9%)
  other arithmetic  14.9 us (6%)
  between operations  13.2 us (5%)
  starting transfers between devices  3.71 us (2%)
    all_gather x2, waiting for transfers between devices, multiply(): lax.all_gather(operand, 'row', axis=0, tiled=True)  92.2 us
    all_gather x1, waiting for transfers between devices, body(): panel = lax.all_gather(rows_done, 'col', axis=1, tiled=True)  57.5 us
    dot_general x2, matrix products, multiply(): jnp.dot(panel, lax.all_gather(operand, 'row', axis=0, tiled=True), prefer...  20.9 us
    mul x4, local copies, waits for them, and re-layouts, apply_pattern(): blocks * pattern[:, None, :, None].astype(matrix.dtype)  18 us
    mul x2, other arithmetic, apply_pattern(): blocks * pattern[:, None, :, None].astype(matrix.dtype)  7.87 us
    ppermute x2, waiting for transfers between devices, shifted(): return lax.ppermute(block, axis, route)  6.51 us
    all_gather x1, local copies, waits for them, and re-layouts, body(): panel = lax.all_gather(rows_done, 'col', axis=1, tiled=True)  6.48 us
    gather x1, local copies, waits for them, and re-layouts, body(): jnp.take(panel.reshape(panel.shape[0], total_blocks, BLK), source, axis=1)  5.48 us
  transfers between devices with their start and end apart: 5, of which 5 were waited for; matrix products, arithmetic and copies ran while one was open for 17% of the time, Pallas kernels for 0%

commit v1 on v0

v1 whole, which is shorter than its diff:
```python
import functools
import jax
import jax.numpy as jnp
from jax import lax
from jax.experimental import pallas as pl
from jax.experimental.pallas import tpu as pltpu
from jax.sharding import PartitionSpec as P

BLK = 64
CAP = 2
Q = 4
NT = 256
MESH = pl.DeviceIdType.MESH


def kernel(n, m, idx, den, ham, dmask, hmask, lanes, out, stack, pack, hfull, lbuf, fbuf, *rest):
    raws = rest[:Q]
    mig_s, mig_r, z_s, z_r, h_s, h_r, f_s, f_r = rest[Q:]
    me = lax.axis_index("row")
    zz = lax.axis_index("col")
    ext, _, width = den.shape
    rows = ext * BLK
    pairs = width // (2 * BLK)
    sub = rows // Q
    per = sub // BLK
    up, down = lax.rem(me + 1, n), lax.rem(me + n - 1, n)

    barrier = pltpu.get_barrier_semaphore()
    for p in range(1, n):
        pl.semaphore_signal(barrier, inc=1, device_id={"row": lax.rem(me + p, n)}, device_id_type=MESH)

    @pl.when(zz > 0)
    def _():
        pl.semaphore_signal(barrier, inc=1, device_id={"col": zz - 1}, device_id_type=MESH)

    @pl.when(zz < m - 1)
    def _():
        pl.semaphore_signal(barrier, inc=1, device_id={"col": zz + 1}, device_id_type=MESH)

    for side in range(2):
        for k in range(CAP):
            pack[side, k] = den[idx[side * CAP + k]]

    pl.semaphore_wait(barrier, n - 1 + (zz > 0).astype(jnp.int32) + (zz < m - 1).astype(jnp.int32))

    migrants = []
    for side, target in enumerate((up, down)):
        c = pltpu.make_async_remote_copy(
            src_ref=pack.at[side],
            dst_ref=stack.at[pl.ds(ext + side * CAP, CAP)],
            send_sem=mig_s.at[side],
            recv_sem=mig_r.at[side],
            device_id={"row": target},
            device_id_type=MESH,
        )
        c.start()
        migrants.append(c)

    for i in range(ext):
        s = pl.ds(i * BLK, BLK)
        hfull[me, s, :] = (ham[s, :].astype(jnp.float32) * hmask[pl.ds(i, 1), :]).astype(jnp.bfloat16)
    for i in range(ext):
        stack[i] = den[i]

    class Gather:
        def __init__(self, view, size, ss, rs):
            self.view, self.size, self.ss, self.rs = view, size, ss, rs
            self.sent = []
            y, x, k = me // 4, lax.rem(me // 2, 2), lax.rem(me, 2)
            self.X = y * 4 + (1 - x) * 2 + k
            self.Y = (1 - y) * 4 + x * 2 + k
            self.D = (1 - y) * 4 + (1 - x) * 2 + k
            self.C = y * 4 + x * 2 + (1 - k)
            self.half = size // 2

        def other(self, slot):
            return slot + 1 - 2 * lax.rem(slot, 2)

        def copy(self, idx, slot, lo, size, target):
            return pltpu.make_async_remote_copy(
                src_ref=self.view(slot, lo, size),
                dst_ref=self.view(slot, lo, size),
                send_sem=self.ss(idx),
                recv_sem=self.rs(idx),
                device_id={"row": target},
                device_id_type=MESH,
            )

        def send(self, *args):
            c = self.copy(*args)
            c.start()
            self.sent.append(c)

        def recv(self, idx, slot, lo, size):
            self.copy(idx, slot, lo, size, self.other(me) if n == 8 else up).wait_recv()

        def start(self):
            h, size = self.half, self.size
            if n != 8:
                for p in range(1, n):
                    self.send(p - 1, me, 0, size, lax.rem(me + p, n))
                return
            self.send(0, me, 0, h, self.X)
            self.send(3, me, h, h, self.Y)
            self.send(1, me, h, h, self.X)
            self.send(2, me, 0, h, self.Y)
            self.send(6, me, 0, size, self.C)

        def turn(self):
            if n != 8:
                return
            h = self.half
            self.recv(0, self.X, 0, h)
            self.send(4, self.X, 0, h, self.Y)
            self.recv(3, self.Y, h, h)
            self.send(5, self.Y, h, h, self.X)

        def share(self):
            if n != 8:
                return
            h, size = self.half, self.size
            self.recv(1, self.X, h, h)
            self.send(7, self.X, 0, size, self.C)
            self.recv(2, self.Y, 0, h)
            self.send(8, self.Y, 0, size, self.C)

        def finish(self):
            h, size = self.half, self.size
            if n != 8:
                for p in range(1, n):
                    self.recv(p - 1, lax.rem(me + n - p, n), 0, size)
                return
            self.recv(4, self.D, 0, h)
            self.recv(5, self.D, h, h)
            self.send(9, self.D, 0, size, self.C)
            for idx, slot in ((6, self.C), (7, self.other(self.X)), (8, self.other(self.Y)), (9, self.other(self.D))):
                self.recv(idx, slot, 0, size)

        def drain(self):
            for c in self.sent:
                c.wait_send()

    gh = Gather(lambda s, lo, size: hfull.at[s, pl.ds(lo, size), :], rows, lambda i: h_s.at[i], lambda i: h_r.at[i])
    gh.start()

    for c in migrants:
        c.wait_recv()
    for i in range(ext):
        block = stack[idx[2 * CAP + i]]
        for t in range(pairs):
            raws[i // per][zz * pairs + t, pl.ds((i % per) * BLK, BLK), :] = block[:, t * 2 * BLK:(t + 1) * 2 * BLK]

    def zcopy(d, q, dist, tile):
        ref = raws[q].at[pl.ds(tile * pairs, pairs)]
        return pltpu.make_async_remote_copy(
            src_ref=ref,
            dst_ref=ref,
            send_sem=z_s.at[d, q, dist],
            recv_sem=z_r.at[d, q, dist],
            device_id={"col": zz - 1 if d == 0 else zz + 1},
            device_id_type=MESH,
        )

    def zown(q):
        for d in range(2):
            @pl.when(zz > 0 if d == 0 else zz < m - 1)
            def _():
                zcopy(d, q, 0, zz).start()

    def zstep(q, dist):
        for d in range(2):
            tile = zz + dist if d == 0 else zz - dist
            there = tile < m if d == 0 else tile >= 0

            @pl.when(there)
            def _():
                zcopy(d, q, dist - 1, tile).wait_recv()

            if dist < m - 1:
                @pl.when(there & (zz > 0 if d == 0 else zz < m - 1))
                def _():
                    zcopy(d, q, dist, tile).start()

    def zdrain():
        for q in range(Q):
            for d in range(2):
                for dist in range(m - 1):
                    tile = zz + dist if d == 0 else zz - dist
                    there = (tile < m if d == 0 else tile >= 0) & (zz > 0 if d == 0 else zz < m - 1)

                    @pl.when(there)
                    def _():
                        zcopy(d, q, dist, tile).wait_send()

    def order(q):
        for c in range(Q):
            @pl.loop(0, n)
            def _(r):
                j = 2 * CAP + ext + r * ext + c * per
                a = raws[q][idx[j]].astype(jnp.float32)
                b = raws[q][idx[j + 1]].astype(jnp.float32)
                cols = pl.ds(pl.multiple_of(r * sub, sub), sub)
                v = a * lanes[c, 0:1, cols] + pltpu.roll(a, BLK, 1) * lanes[c, 1:2, cols]
                v += pltpu.roll(b, BLK, 1) * lanes[c, 2:3, cols] + b * lanes[c, 3:4, cols]
                for i in range(per):
                    w = v[i * BLK:(i + 1) * BLK] * dmask[c, pl.ds(q * per + i, 1), cols]
                    lbuf[c, pl.ds(q * sub + i * BLK, BLK), cols] = w.astype(jnp.bfloat16)

    def first(q):
        @pl.loop(0, width // NT)
        def _(t):
            cols = pl.ds(pl.multiple_of(t * NT, NT), NT)
            total = jnp.zeros((sub, NT), jnp.float32)
            for c in range(Q):
                h = hfull[:, pl.ds(c * sub, sub), cols].reshape(n * sub, NT)
                total += jnp.dot(lbuf[c, pl.ds(q * sub, sub), :], h, preferred_element_type=jnp.float32)
            fbuf[q, me, :, cols] = total.astype(jnp.bfloat16)

    def second(q):
        @pl.loop(0, width // NT)
        def _(t):
            cols = pl.ds(pl.multiple_of(t * NT, NT), NT)
            f = fbuf[q, :, :, cols].reshape(n * sub, NT)
            total = jnp.dot(lbuf[q], f, preferred_element_type=jnp.float32)
            if q > 0:
                total += out[:, cols]
            if q == Q - 1:
                own = fbuf[:, me, :, cols].reshape(rows, NT).astype(jnp.float32)
                total = 3.0 * own - 2.0 * total
            out[:, cols] = total

    gf = [
        Gather(
            (lambda q: lambda s, lo, size: fbuf.at[q, s, pl.ds(lo, size), :])(q),
            sub,
            (lambda q: lambda i: f_s.at[q, i])(q),
            (lambda q: lambda i: f_r.at[q, i])(q),
        )
        for q in range(Q)
    ]

    zown(0)
    zown(1)
    zstep(0, 1)
    gh.turn()
    for dist in range(2, m):
        zstep(0, dist)
    zown(2)
    zstep(1, 1)
    order(0)
    gh.share()
    for dist in range(2, m):
        zstep(1, dist)
    zown(3)
    zstep(2, 1)
    order(1)
    gh.finish()
    first(0)
    gf[0].start()
    first(1)
    gf[1].start()
    gf[0].turn()
    for dist in range(2, m):
        zstep(2, dist)
    zstep(3, 1)
    order(2)
    first(2)
    gf[2].start()
    gf[1].turn()
    gf[0].share()
    gf[0].finish()
    gf[1].share()
    gf[1].finish()
    gf[2].turn()
    for dist in range(2, m):
        zstep(3, dist)
    order(3)
    first(3)
    gf[3].start()
    gf[2].share()
    second(0)
    gf[3].turn()
    gf[2].finish()
    second(1)
    gf[3].share()
    second(2)
    gf[3].finish()
    second(3)

    for c in migrants:
        c.wait_send()
    zdrain()
    gh.drain()
    for g in gf:
        g.drain()


def body(density, hamiltonian, density_pattern, ham_pattern, source):
    n, m = lax.axis_size("row"), lax.axis_size("col")
    rows, width = density.shape
    ext, wide = rows // BLK, width // BLK
    per = ext // Q
    sub = rows // Q
    me, zz = lax.axis_index("row"), lax.axis_index("col")
    rp = lax.dynamic_slice_in_dim(density_pattern, me * ext, ext, 0).astype(jnp.float32)
    rp = rp.reshape(ext, n, Q, per).transpose(2, 0, 1, 3)
    dmask = jnp.broadcast_to(rp[..., None], (Q, ext, n, per, BLK)).reshape(Q, ext, n * sub)
    hp = lax.dynamic_slice(ham_pattern, (me * ext, zz * wide), (ext, wide)).astype(jnp.float32)
    hmask = jnp.broadcast_to(hp[..., None], (ext, wide, BLK)).reshape(ext, width)
    places = jnp.arange(ext, dtype=jnp.int32)
    up, down = (me + 1) % n, (me - 1) % n

    def mine(target):
        return lax.dynamic_slice_in_dim(source, target * ext, ext)

    def rank(hit):
        before = places[None, :] < places[:, None]
        return jnp.sum(jnp.where(before & hit[None, :], 1, 0), axis=1)

    picks = []
    for target in (up, down):
        olds = mine(target)
        hit = olds // ext == me
        order = rank(hit)
        for k in range(CAP):
            picks.append(jnp.sum(jnp.where(hit & (order == k), olds % ext, 0)).reshape(1))
    olds = mine(me)
    lower, upper = olds // ext == down, olds // ext == up
    assembled = jnp.where(
        lower, ext + rank(lower), jnp.where(upper, ext + CAP + rank(upper), olds % ext)
    )
    idx = jnp.concatenate(picks + [assembled, source // 2]).astype(jnp.int32)
    odd = (source % 2).astype(jnp.float32).reshape(n, Q, per).transpose(1, 0, 2)
    zero = jnp.zeros_like(odd[..., 0])
    halves = [
        (1 - odd[..., 0], zero),
        (odd[..., 0], zero),
        (zero, 1 - odd[..., 1]),
        (zero, odd[..., 1]),
    ]
    lanes = jnp.stack([jnp.stack(h, axis=-1) for h in halves], axis=1)
    lanes = jnp.broadcast_to(lanes[..., None], lanes.shape + (BLK,)).reshape(Q, 4, n * sub)
    sems = max(10, n - 1)
    dma = pltpu.SemaphoreType.DMA
    bf = jnp.bfloat16
    vm = pl.BlockSpec(memory_space=pltpu.VMEM)
    return pl.pallas_call(
        functools.partial(kernel, n, m),
        out_shape=jax.ShapeDtypeStruct((rows, width), jnp.float32),
        in_specs=[pl.BlockSpec(memory_space=pltpu.SMEM), vm, vm, vm, vm, vm],
        out_specs=vm,
        scratch_shapes=[
            pltpu.VMEM((ext + 2 * CAP, BLK, width), bf),
            pltpu.VMEM((2, CAP, BLK, width), bf),
            pltpu.VMEM((n, rows, width), bf),
            pltpu.VMEM((Q, rows, n * sub), bf),
            pltpu.VMEM((Q, n, sub, width), bf),
        ]
        + [pltpu.VMEM((m * width // (2 * BLK), sub, 2 * BLK), bf) for _ in range(Q)]
        + [
            dma((2,)), dma((2,)),
            dma((2, Q, m)), dma((2, Q, m)),
            dma((sems,)), dma((sems,)),
            dma((Q, sems)), dma((Q, sems)),
        ],
        compiler_params=pltpu.CompilerParams(
            collective_id=0, has_side_effects=True, vmem_limit_bytes=(60 if n > 8 else 48) * 1024 * 1024
        ),
        cost_estimate=pl.CostEstimate(
            flops=4 * rows * n * rows * width, bytes_accessed=8 * rows * width, transcendentals=0
        ),
    )(idx, density.reshape(ext, BLK, width), hamiltonian, dmask, hmask, lanes)


def solution(mesh):
    return jax.shard_map(
        body,
        mesh=mesh,
        in_specs=(P("row", "col"), P("row", "col"), P(), P(), P()),
        out_specs=P("row", "col"),
        check_vma=False,
    )
```

time: 244 us -> 122 us (0.50)
  waiting for transfers between devices: 156 us -> 0 us
  Pallas kernels: 0 us -> 110 us
  local copies, waits for them, and re-layouts: 34.6 us -> 6.12 us
  matrix products: 20.9 us -> 0 us
  between operations: 13.2 us -> 0.07 us
  other arithmetic: 14.9 us -> 5.63 us
  starting transfers between devices: 3.71 us -> 0 us
    all_gather x3 -> x0, waiting for transfers between devices: 150 us -> none  [the longest x2 92.2 us: multiply(): lax.all_gather(operand, 'row', axis=0, tiled=True)]
    pallas_call x0 -> x1, Pallas kernels: none -> 110 us  [body(): pl.pallas_call(functools.partial(kernel, n, m), out_shape=jax.ShapeDtypeS...]
    dot_general x2 -> x0, matrix products: 20.9 us -> none  [multiply(): jnp.dot(panel, lax.all_gather(operand, 'row', axis=0, tiled=True), prefer...]
    mul x4 -> x0, local copies, waits for them, and re-layouts: 18 us -> none  [apply_pattern(): blocks * pattern[:, None, :, None].astype(matrix.dtype)]
    gather x4 -> x0, local copies, waits for them, and re-layouts: 9.68 us -> none  [the longest x1 5.48 us: body(): jnp.take(panel.reshape(panel.shape[0], total_blocks, BLK), source, axis=1)]
    mul x4 -> x0, other arithmetic: 8.06 us -> none  [the longest x2 7.87 us: apply_pattern(): blocks * pattern[:, None, :, None].astype(matrix.dtype)]
    ppermute x2 -> x0, waiting for transfers between devices: 6.51 us -> none  [shifted(): return lax.ppermute(block, axis, route)]
    all_gather x1 -> x0, local copies, waits for them, and re-layouts: 6.48 us -> none  [body(): panel = lax.all_gather(rows_done, 'col', axis=1, tiled=True)]
  transfers between devices with their start and end apart: 5 -> 0, of which waited for: 5 -> 0; matrix products, arithmetic and copies ran while one was open for 17% -> 0% of each run, Pallas kernels for 0% -> 0%
where the time goes in v1:
time: 122 us
  Pallas kernels  110 us (90%)
  local copies, waits for them, and re-layouts  6.12 us (5%)
  other arithmetic  5.63 us (5%)
    pallas_call x1, Pallas kernels, body(): pl.pallas_call(functools.partial(kernel, n, m), out_shape=jax.ShapeDtypeS...  110 us
    concatenate x1, local copies, waits for them, and re-layouts, body(): idx = jnp.concatenate(picks + [assembled, source // 2]).astype(jnp.int32)  2.61 us

profile of v1, /device:TPU:0, one launch (start us, length us, event | category | flops | bytes accessed | tf_op | source)
XLA Modules:
  0.0 121.6 jit_solution(13514073700940156072)
XLA Ops:
  0.0 0.0 copy-start
  0.0 0.9 broadcast_compare_fusion
  0.9 0.1 select_reduce_fusion.1
  1.1 0.1 select_reduce_fusion.3
  1.2 0.7 fusion.8
  1.9 0.1 select_reduce_fusion
  2.1 0.7 fusion.5
  2.8 0.7 fusion.10
  3.5 0.7 fusion.6
  4.1 2.6 %concatenate.3.idx = s32[76]{0:T(128)S(1)} concatenate(s32[1]{0:T(128)} %bitcast, s32[1]{0:T(128)} %bitcast.1, s32[1]{0:T(128)} %bitcast.2, s32[1]{0:T(128)} %bitcast.3, s32[8]{0:T(128)S(1)} %fusion.5, s32[64]{0:T(128)S(1)} %get-tuple-element.19), dimensions={0} | concatenate | bytes 608 | tf_op jit(solution)/shard_map/concatenate | solution.py:332
  6.7 0.8 dynamic-slice_convert_fusion
  7.5 0.0 copy-done
  7.5 0.1 reshape.45
  7.6 0.7 broadcast_select_fusion
  8.3 0.1 copy.22
  8.4 0.1 copy.26
  8.5 0.1 slice_subtract_fusion
  8.6 0.1 copy.27
  8.7 0.1 copy.28
  8.8 0.1 copy.29
  8.9 0.2 copy.25
  9.1 0.1 broadcast_in_dim.28
  9.1 0.1 reshape.44.hmask
  9.2 0.2 broadcast_in_dim.29
  9.4 0.2 reshape.46.lanes
  9.6 0.3 copy.20
  9.9 0.3 broadcast_in_dim.27
  10.2 0.3 reshape.43.dmask
  10.5 0.0 copy-done.2
  10.5 0.0 copy-done.1
  10.5 109.8 %shard_map.55 = f32[512,1024]{1,0:T(8,128)S(1)} custom-call(s32[76]{0:T(128)S(1)} %concatenate.3.idx, bf16[8,64,1024]{2,1,0:T(8,128)(2,1)S(1)} %bitcast.17, bf16[512,1024]{1,0:T(8,128)(2,1)S(1)} %copy-done.2, f32[4,8,1024]{2,1,0:T(8,128)S(1)} %reshape.43.dmask, f32[8,1024]{1,0:T(8,128)S(1)} %reshape.44.hmask, f32[4,4,1024]{2,1,0:T(4,128)S(1)} %reshape.46.lanes), custom_call_target="tpu_custom_call" | custom-call | flops 8589934592 | bytes 4194304 | tf_op jit(solution)/shard_map/pallas_call | solution.py:347
  120.3 1.3 %copy.31 = f32[512,1024]{1,0:T(8,128)} copy(f32[512,1024]{1,0:T(8,128)S(1)} %shard_map.55) | data formatting | bytes 4194304
  (8 shorter events, 0.0 us)
Async XLA Ops:
  0.0 7.5 %copy-start = (s32[64,64]{1,0:T(8,128)S(1)}, s32[64,64]{1,0:T(8,128)}, u32[]{:S(2)}) copy-start(s32[64,64]{1,0:T(8,128)} %param.7) | copy-start | bytes 49156
  0.0 10.5 %copy-start.2 = (bf16[512,1024]{1,0:T(8,128)(2,1)S(1)}, bf16[512,1024]{1,0:T(8,128)(2,1)}, u32[]{:S(2)}) copy-start(bf16[512,1024]{1,0:T(8,128)(2,1)} %ham.1) | copy-start | bytes 3145732
  0.0 10.5 %copy-start.1 = (bf16[512,1024]{1,0:T(8,128)(2,1)S(1)}, bf16[512,1024]{1,0:T(8,128)(2,1)}, u32[]{:S(2)}) copy-start(bf16[512,1024]{1,0:T(8,128)(2,1)} %param.5) | copy-start | bytes 3145732

commit v2 on v1

--- a/solution.py
+++ b/solution.py
@@ -13,7 +13,7 @@
 MESH = pl.DeviceIdType.MESH
 
 
-def kernel(n, m, idx, den, ham, dmask, hmask, lanes, out, stack, pack, hfull, lbuf, fbuf, *rest):
+def kernel(n, m, src, dpat, hpat, den, ham, out, stack, pack, hfull, lbuf, fbuf, *rest):
     raws = rest[:Q]
     mig_s, mig_r, z_s, z_r, h_s, h_r, f_s, f_r = rest[Q:]
     me = lax.axis_index("row")
@@ -37,9 +37,17 @@
     def _():
         pl.semaphore_signal(barrier, inc=1, device_id={"col": zz + 1}, device_id_type=MESH)
 
-    for side in range(2):
+    for side, target in enumerate((up, down)):
+        count = jnp.int32(0)
+        picks = [jnp.int32(0)] * CAP
+        for i in range(ext):
+            a = src[target * ext + i]
+            hit = (lax.div(a, ext) == me).astype(jnp.int32)
+            for k in range(CAP):
+                picks[k] = picks[k] + hit * (count == k).astype(jnp.int32) * lax.rem(a, ext)
+            count = count + hit
         for k in range(CAP):
-            pack[side, k] = den[idx[side * CAP + k]]
+            pack[side, k] = den[picks[k]]
 
     pl.semaphore_wait(barrier, n - 1 + (zz > 0).astype(jnp.int32) + (zz < m - 1).astype(jnp.int32))
 
@@ -56,9 +64,23 @@
         c.start()
         migrants.append(c)
 
-    for i in range(ext):
-        s = pl.ds(i * BLK, BLK)
-        hfull[me, s, :] = (ham[s, :].astype(jnp.float32) * hmask[pl.ds(i, 1), :]).astype(jnp.bfloat16)
+    lane = lax.broadcasted_iota(jnp.int32, (1, 2 * BLK), 1)
+    low = (lane < BLK).astype(jnp.float32)
+    high = 1.0 - low
+
+    def keep(p0, p1):
+        return low * p0.astype(jnp.float32) + high * p1.astype(jnp.float32)
+
+    @pl.loop(0, ext)
+    def _(i):
+        for t in range(pairs):
+            j = zz * pairs * 2 + t * 2
+            s = pl.ds(pl.multiple_of(i * BLK, BLK), BLK)
+            cols = pl.ds(t * 2 * BLK, 2 * BLK)
+            row = me * ext + i
+            w = ham[s, cols].astype(jnp.float32) * keep(hpat[row, j], hpat[row, j + 1])
+            hfull[me, s, cols] = w.astype(jnp.bfloat16)
+
     for i in range(ext):
         stack[i] = den[i]
 
@@ -145,8 +167,15 @@
 
     for c in migrants:
         c.wait_recv()
+    nlow, nupp = jnp.int32(0), jnp.int32(0)
     for i in range(ext):
-        block = stack[idx[2 * CAP + i]]
+        a = src[me * ext + i]
+        home = lax.div(a, ext)
+        lower, upper = (home == down).astype(jnp.int32), (home == up).astype(jnp.int32)
+        pick = lower * (ext + jnp.minimum(nlow, CAP - 1)) + upper * (ext + CAP + jnp.minimum(nupp, CAP - 1)) + (1 - lower - upper) * lax.rem(a, ext)
+        nlow = nlow + lower
+        nupp = nupp + upper
+        block = stack[pick]
         for t in range(pairs):
             raws[i // per][zz * pairs + t, pl.ds((i % per) * BLK, BLK), :] = block[:, t * 2 * BLK:(t + 1) * 2 * BLK]
 
@@ -196,14 +225,17 @@
         for c in range(Q):
             @pl.loop(0, n)
             def _(r):
-                j = 2 * CAP + ext + r * ext + c * per
-                a = raws[q][idx[j]].astype(jnp.float32)
-                b = raws[q][idx[j + 1]].astype(jnp.float32)
+                j = r * ext + c * per
+                s0, s1 = src[j], src[j + 1]
+                e0, e1 = lax.rem(s0, 2).astype(jnp.float32), lax.rem(s1, 2).astype(jnp.float32)
+                a = raws[q][lax.div(s0, 2)].astype(jnp.float32)
+                b = raws[q][lax.div(s1, 2)].astype(jnp.float32)
                 cols = pl.ds(pl.multiple_of(r * sub, sub), sub)
-                v = a * lanes[c, 0:1, cols] + pltpu.roll(a, BLK, 1) * lanes[c, 1:2, cols]
-                v += pltpu.roll(b, BLK, 1) * lanes[c, 2:3, cols] + b * lanes[c, 3:4, cols]
+                v = a * (low * (1.0 - e0)) + pltpu.roll(a, BLK, 1) * (low * e0)
+                v += pltpu.roll(b, BLK, 1) * (high * (1.0 - e1)) + b * (high * e1)
                 for i in range(per):
-                    w = v[i * BLK:(i + 1) * BLK] * dmask[c, pl.ds(q * per + i, 1), cols]
+                    row = me * ext + q * per + i
+                    w = v[i * BLK:(i + 1) * BLK] * keep(dpat[row, j], dpat[row, j + 1])
                     lbuf[c, pl.ds(q * sub + i * BLK, BLK), cols] = w.astype(jnp.bfloat16)
 
     def first(q):
@@ -298,56 +330,17 @@
 def body(density, hamiltonian, density_pattern, ham_pattern, source):
     n, m = lax.axis_size("row"), lax.axis_size("col")
     rows, width = density.shape
-    ext, wide = rows // BLK, width // BLK
-    per = ext // Q
+    ext = rows // BLK
     sub = rows // Q
-    me, zz = lax.axis_index("row"), lax.axis_index("col")
-    rp = lax.dynamic_slice_in_dim(density_pattern, me * ext, ext, 0).astype(jnp.float32)
-    rp = rp.reshape(ext, n, Q, per).transpose(2, 0, 1, 3)
-    dmask = jnp.broadcast_to(rp[..., None], (Q, ext, n, per, BLK)).reshape(Q, ext, n * sub)
-    hp = lax.dynamic_slice(ham_pattern, (me * ext, zz * wide), (ext, wide)).astype(jnp.float32)
-    hmask = jnp.broadcast_to(hp[..., None], (ext, wide, BLK)).reshape(ext, width)
-    places = jnp.arange(ext, dtype=jnp.int32)
-    up, down = (me + 1) % n, (me - 1) % n
-
-    def mine(target):
-        return lax.dynamic_slice_in_dim(source, target * ext, ext)
-
-    def rank(hit):
-        before = places[None, :] < places[:, None]
-        return jnp.sum(jnp.where(before & hit[None, :], 1, 0), axis=1)
-
-    picks = []
-    for target in (up, down):
-        olds = mine(target)
-        hit = olds // ext == me
-        order = rank(hit)
-        for k in range(CAP):
-            picks.append(jnp.sum(jnp.where(hit & (order == k), olds % ext, 0)).reshape(1))
-    olds = mine(me)
-    lower, upper = olds // ext == down, olds // ext == up
-    assembled = jnp.where(
-        lower, ext + rank(lower), jnp.where(upper, ext + CAP + rank(upper), olds % ext)
-    )
-    idx = jnp.concatenate(picks + [assembled, source // 2]).astype(jnp.int32)
-    odd = (source % 2).astype(jnp.float32).reshape(n, Q, per).transpose(1, 0, 2)
-    zero = jnp.zeros_like(odd[..., 0])
-    halves = [
-        (1 - odd[..., 0], zero),
-        (odd[..., 0], zero),
-        (zero, 1 - odd[..., 1]),
-        (zero, odd[..., 1]),
-    ]
-    lanes = jnp.stack([jnp.stack(h, axis=-1) for h in halves], axis=1)
-    lanes = jnp.broadcast_to(lanes[..., None], lanes.shape + (BLK,)).reshape(Q, 4, n * sub)
     sems = max(10, n - 1)
     dma = pltpu.SemaphoreType.DMA
     bf = jnp.bfloat16
+    sm = pl.BlockSpec(memory_space=pltpu.SMEM)
     vm = pl.BlockSpec(memory_space=pltpu.VMEM)
     return pl.pallas_call(
         functools.partial(kernel, n, m),
         out_shape=jax.ShapeDtypeStruct((rows, width), jnp.float32),
-        in_specs=[pl.BlockSpec(memory_space=pltpu.SMEM), vm, vm, vm, vm, vm],
+        in_specs=[sm, sm, sm, vm, vm],
         out_specs=vm,
         scratch_shapes=[
             pltpu.VMEM((ext + 2 * CAP, BLK, width), bf),
@@ -369,7 +362,7 @@
         cost_estimate=pl.CostEstimate(
             flops=4 * rows * n * rows * width, bytes_accessed=8 * rows * width, transcendentals=0
         ),
-    )(idx, density.reshape(ext, BLK, width), hamiltonian, dmask, hmask, lanes)
+    )(source, density_pattern, ham_pattern, density.reshape(ext, BLK, width), hamiltonian)
 
 
 def solution(mesh):

time: 122 us -> 117 us (0.959)
  other arithmetic: 5.63 us -> 0 us
    unnamed x11, local copies, waits for them, and re-layouts: 1.72 us -> 5.94 us
    concatenate x1 -> x0, local copies, waits for them, and re-layouts: 2.61 us -> none  [body(): idx = jnp.concatenate(picks + [assembled, source // 2]).astype(jnp.int32)]
    reduce_sum x5 -> x0, other arithmetic: 1.77 us -> none  [the longest x2 1.39 us: body(): jnp.sum(jnp.where(hit & (order == k), olds % ext, 0)).reshape(1)]
    convert_element_type x3 -> x0, other arithmetic: 1.43 us -> none  [the longest x1 0.76 us: body(): lax.dynamic_slice(ham_pattern, (me * ext, zz * wide), (ext, wide))]
where the time goes in v2:
time: 117 us
  Pallas kernels  111 us (95%)
  local copies, waits for them, and re-layouts  5.94 us (5%)
    pallas_call x1, Pallas kernels, body(): pl.pallas_call(functools.partial(kernel, n, m), out_shape=jax.ShapeDtypeS...  111 us
    unnamed x11, local copies, waits for them, and re-layouts  5.94 us

profile of v2, /device:TPU:0, one launch (start us, length us, event | category | flops | bytes accessed | tf_op | source)
XLA Modules:
  0.0 116.7 jit_solution(8203554473263268533)
XLA Ops:
  0.0 0.0 copy-start
  0.0 1.2 %copy-done = bf16[512,1024]{1,0:T(8,128)(2,1)S(1)} copy-done((bf16[512,1024]{1,0:T(8,128)(2,1)S(1)}, bf16[512,1024]{1,0:T(8,128)(2,1)}, u32[]{:S(2)}) %copy-start) | copy-done | bytes 1048600
  1.2 0.0 copy-start.1
  1.2 1.2 %copy-done.1 = bf16[512,1024]{1,0:T(8,128)(2,1)S(1)} copy-done((bf16[512,1024]{1,0:T(8,128)(2,1)S(1)}, bf16[512,1024]{1,0:T(8,128)(2,1)}, u32[]{:S(2)}) %copy-start.1) | copy-done | bytes 1048600
  2.5 0.0 copy-start.2
  2.5 0.8 copy-done.2
  3.2 0.0 copy-start.3
  3.2 0.8 copy-done.3
  4.0 0.0 copy-start.4
  4.0 0.7 copy-done.4
  4.6 110.8 %shard_map.55 = f32[512,1024]{1,0:T(8,128)S(1)} custom-call(s32[64]{0:T(128)S(1)} %copy-done.4, s32[64,64]{1,0:T(8,128)S(1)} %copy-done.2, s32[64,64]{1,0:T(8,128)S(1)} %copy-done.3, bf16[8,64,1024]{2,1,0:T(8,128)(2,1)S(1)} %bitcast.1, bf16[512,1024]{1,0:T(8,128)(2,1)S(1)} %copy-done.1), custom_call_target="tpu_custom_call" | custom-call | flops 8589934592 | bytes 4194304 | tf_op jit(solution)/shard_map/pallas_call | solution.py:340
  115.4 1.3 %copy.7 = f32[512,1024]{1,0:T(8,128)} copy(f32[512,1024]{1,0:T(8,128)S(1)} %shard_map.55) | data formatting | bytes 4194304
Async XLA Ops:
  0.0 1.2 %copy-start = (bf16[512,1024]{1,0:T(8,128)(2,1)S(1)}, bf16[512,1024]{1,0:T(8,128)(2,1)}, u32[]{:S(2)}) copy-start(bf16[512,1024]{1,0:T(8,128)(2,1)} %param.5) | copy-start | bytes 3145732
  1.2 1.2 %copy-start.1 = (bf16[512,1024]{1,0:T(8,128)(2,1)S(1)}, bf16[512,1024]{1,0:T(8,128)(2,1)}, u32[]{:S(2)}) copy-start(bf16[512,1024]{1,0:T(8,128)(2,1)} %ham.1) | copy-start | bytes 3145732
  2.5 0.8 copy-start.2
  3.2 0.8 copy-start.3
  4.0 0.7 copy-start.4

commit v3 on v2

--- a/solution.py
+++ b/solution.py
@@ -13,9 +13,9 @@
 MESH = pl.DeviceIdType.MESH
 
 
-def kernel(n, m, src, dpat, hpat, den, ham, out, stack, pack, hfull, lbuf, fbuf, *rest):
+def kernel(n, m, src, dpat, hpat, den_hbm, ham_hbm, out, den, ham, stack, pack, hfull, lbuf, fbuf, *rest):
     raws = rest[:Q]
-    mig_s, mig_r, z_s, z_r, h_s, h_r, f_s, f_r = rest[Q:]
+    mig_s, mig_r, z_s, z_r, h_s, h_r, f_s, f_r, in_s = rest[Q:]
     me = lax.axis_index("row")
     zz = lax.axis_index("col")
     ext, _, width = den.shape
@@ -24,6 +24,13 @@
     sub = rows // Q
     per = sub // BLK
     up, down = lax.rem(me + 1, n), lax.rem(me + n - 1, n)
+    loads = [
+        pltpu.make_async_copy(den_hbm, den, in_s.at[0]),
+        pltpu.make_async_copy(ham_hbm, ham, in_s.at[1]),
+        pltpu.make_async_copy(den_hbm, stack.at[pl.ds(0, ext)], in_s.at[2]),
+    ]
+    for c in loads:
+        c.start()
 
     barrier = pltpu.get_barrier_semaphore()
     for p in range(1, n):
@@ -37,6 +44,7 @@
     def _():
         pl.semaphore_signal(barrier, inc=1, device_id={"col": zz + 1}, device_id_type=MESH)
 
+    loads[0].wait()
     for side, target in enumerate((up, down)):
         count = jnp.int32(0)
         picks = [jnp.int32(0)] * CAP
@@ -64,6 +72,7 @@
         c.start()
         migrants.append(c)
 
+    loads[1].wait()
     lane = lax.broadcasted_iota(jnp.int32, (1, 2 * BLK), 1)
     low = (lane < BLK).astype(jnp.float32)
     high = 1.0 - low
@@ -81,8 +90,7 @@
             w = ham[s, cols].astype(jnp.float32) * keep(hpat[row, j], hpat[row, j + 1])
             hfull[me, s, cols] = w.astype(jnp.bfloat16)
 
-    for i in range(ext):
-        stack[i] = den[i]
+    loads[2].wait()
 
     class Gather:
         def __init__(self, view, size, ss, rs):
@@ -153,10 +161,13 @@
                     self.recv(p - 1, lax.rem(me + n - p, n), 0, size)
                 return
             self.recv(4, self.D, 0, h)
+            self.send(9, self.D, 0, h, self.C)
             self.recv(5, self.D, h, h)
-            self.send(9, self.D, 0, size, self.C)
-            for idx, slot in ((6, self.C), (7, self.other(self.X)), (8, self.other(self.Y)), (9, self.other(self.D))):
+            self.send(10, self.D, h, h, self.C)
+            for idx, slot in ((6, self.C), (7, self.other(self.X)), (8, self.other(self.Y))):
                 self.recv(idx, slot, 0, size)
+            self.recv(9, self.other(self.D), 0, h)
+            self.recv(10, self.other(self.D), h, h)
 
         def drain(self):
             for c in self.sent:
@@ -238,15 +249,16 @@
                     w = v[i * BLK:(i + 1) * BLK] * keep(dpat[row, j], dpat[row, j + 1])
                     lbuf[c, pl.ds(q * sub + i * BLK, BLK), cols] = w.astype(jnp.bfloat16)
 
-    def first(q):
+    def first(q, chunks):
         @pl.loop(0, width // NT)
         def _(t):
             cols = pl.ds(pl.multiple_of(t * NT, NT), NT)
-            total = jnp.zeros((sub, NT), jnp.float32)
+            total = jnp.zeros((chunks * sub, NT), jnp.float32)
             for c in range(Q):
                 h = hfull[:, pl.ds(c * sub, sub), cols].reshape(n * sub, NT)
-                total += jnp.dot(lbuf[c, pl.ds(q * sub, sub), :], h, preferred_element_type=jnp.float32)
-            fbuf[q, me, :, cols] = total.astype(jnp.bfloat16)
+                total += jnp.dot(lbuf[c, pl.ds(q * sub, chunks * sub), :], h, preferred_element_type=jnp.float32)
+            for i in range(chunks):
+                fbuf[q + i, me, :, cols] = total[i * sub:(i + 1) * sub].astype(jnp.bfloat16)
 
     def second(q):
         @pl.loop(0, width // NT)
@@ -287,33 +299,34 @@
     zstep(2, 1)
     order(1)
     gh.finish()
-    first(0)
+    first(0, 2)
     gf[0].start()
-    first(1)
     gf[1].start()
-    gf[0].turn()
-    for dist in range(2, m):
+    for dist in range(2, m - 1):
         zstep(2, dist)
     zstep(3, 1)
+    zstep(2, m - 1)
+    gf[0].turn()
     order(2)
-    first(2)
+    first(2, 1)
     gf[2].start()
     gf[1].turn()
+    for dist in range(2, m - 1):
+        zstep(3, dist)
+    gf[2].turn()
+    zstep(3, m - 1)
+    order(3)
+    first(3, 1)
+    gf[3].start()
     gf[0].share()
     gf[0].finish()
+    second(0)
     gf[1].share()
     gf[1].finish()
-    gf[2].turn()
-    for dist in range(2, m):
-        zstep(3, dist)
-    order(3)
-    first(3)
-    gf[3].start()
+    gf[3].turn()
+    second(1)
     gf[2].share()
-    second(0)
-    gf[3].turn()
     gf[2].finish()
-    second(1)
     gf[3].share()
     second(2)
     gf[3].finish()
@@ -332,17 +345,20 @@
     rows, width = density.shape
     ext = rows // BLK
     sub = rows // Q
-    sems = max(10, n - 1)
+    sems = max(11, n - 1)
     dma = pltpu.SemaphoreType.DMA
     bf = jnp.bfloat16
     sm = pl.BlockSpec(memory_space=pltpu.SMEM)
+    anywhere = pl.BlockSpec(memory_space=pl.ANY)
     vm = pl.BlockSpec(memory_space=pltpu.VMEM)
     return pl.pallas_call(
         functools.partial(kernel, n, m),
         out_shape=jax.ShapeDtypeStruct((rows, width), jnp.float32),
-        in_specs=[sm, sm, sm, vm, vm],
+        in_specs=[sm, sm, sm, anywhere, anywhere],
         out_specs=vm,
         scratch_shapes=[
+            pltpu.VMEM((ext, BLK, width), bf),
+            pltpu.VMEM((rows, width), bf),
             pltpu.VMEM((ext + 2 * CAP, BLK, width), bf),
             pltpu.VMEM((2, CAP, BLK, width), bf),
             pltpu.VMEM((n, rows, width), bf),
@@ -355,9 +371,10 @@
             dma((2, Q, m)), dma((2, Q, m)),
             dma((sems,)), dma((sems,)),
             dma((Q, sems)), dma((Q, sems)),
+            dma((3,)),
         ],
         compiler_params=pltpu.CompilerParams(
-            collective_id=0, has_side_effects=True, vmem_limit_bytes=(60 if n > 8 else 48) * 1024 * 1024
+            collective_id=0, has_side_effects=True, vmem_limit_bytes=60 * 1024 * 1024
         ),
         cost_estimate=pl.CostEstimate(
             flops=4 * rows * n * rows * width, bytes_accessed=8 * rows * width, transcendentals=0

time: 117 us -> 112 us (0.957)
  local copies, waits for them, and re-layouts: 5.94 us -> 3.16 us
  Pallas kernels: 111 us -> 109 us
    unnamed x11 -> x1, local copies, waits for them, and re-layouts: 5.94 us -> 3.16 us
    pallas_call x1, Pallas kernels: 111 us -> 109 us  [body(): pl.pallas_call(functools.partial(kernel, n, m), out_shape=jax.ShapeDtypeS...]
where the time goes in v3:
time: 112 us
  Pallas kernels  109 us (97%)
  local copies, waits for them, and re-layouts  3.16 us (3%)
    pallas_call x1, Pallas kernels, body(): pl.pallas_call(functools.partial(kernel, n, m), out_shape=jax.ShapeDtypeS...  109 us
    unnamed x1, local copies, waits for them, and re-layouts  3.16 us

profile of v3, /device:TPU:0, one launch (start us, length us, event | category | flops | bytes accessed | tf_op | source)
XLA Modules:
  0.0 112.2 jit_solution(5044076718664961904)
XLA Ops:
  0.0 109.0 %shard_map.55 = f32[512,1024]{1,0:T(8,128)} custom-call(s32[64]{0:T(128)} %src.1, s32[64,64]{1,0:T(8,128)} %dpat.1, s32[64,64]{1,0:T(8,128)} %hpat.1, bf16[8,64,1024]{2,1,0:T(8,128)(2,1)} %bitcast.1, bf16[512,1024]{1,0:T(8,128)(2,1)} %ham_hbm.1), custom_call_target="tpu_custom_call" | custom-call | flops 8589934592 | bytes 4194304 | tf_op jit(solution)/shard_map/pallas_call | solution.py:354
  109.0 3.2 %copy.7 = f32[512,1024]{1,0:T(8,128)} copy(f32[512,1024]{1,0:T(8,128)} %shard_map.55) | data formatting | bytes 4194304

commit v4 on v3

--- a/solution.py
+++ b/solution.py
@@ -80,7 +80,7 @@
     def keep(p0, p1):
         return low * p0.astype(jnp.float32) + high * p1.astype(jnp.float32)
 
-    @pl.loop(0, ext)
+    @pl.loop(0, ext, unroll=2)
     def _(i):
         for t in range(pairs):
             j = zz * pairs * 2 + t * 2
@@ -234,7 +234,7 @@
 
     def order(q):
         for c in range(Q):
-            @pl.loop(0, n)
+            @pl.loop(0, n, unroll=4)
             def _(r):
                 j = r * ext + c * per
                 s0, s1 = src[j], src[j + 1]

time: 112 us -> 110 us (0.982)
  Pallas kernels: 109 us -> 107 us
    pallas_call x1, Pallas kernels: 109 us -> 107 us  [body(): pl.pallas_call(functools.partial(kernel, n, m), out_shape=jax.ShapeDtypeS...]
where the time goes in v4:
time: 110 us
  Pallas kernels  107 us (97%)
  local copies, waits for them, and re-layouts  3.16 us (3%)
    pallas_call x1, Pallas kernels, body(): pl.pallas_call(functools.partial(kernel, n, m), out_shape=jax.ShapeDtypeS...  107 us
    unnamed x1, local copies, waits for them, and re-layouts  3.16 us

profile of v4, /device:TPU:0, one launch (start us, length us, event | category | flops | bytes accessed | tf_op | source)
XLA Modules:
  0.0 110.1 jit_solution(13525616978992339751)
XLA Ops:
  0.0 107.0 %shard_map.55 = f32[512,1024]{1,0:T(8,128)} custom-call(s32[64]{0:T(128)} %src.1, s32[64,64]{1,0:T(8,128)} %dpat.1, s32[64,64]{1,0:T(8,128)} %hpat.1, bf16[8,64,1024]{2,1,0:T(8,128)(2,1)} %bitcast.1, bf16[512,1024]{1,0:T(8,128)(2,1)} %ham_hbm.1), custom_call_target="tpu_custom_call" | custom-call | flops 8589934592 | bytes 4194304 | tf_op jit(solution)/shard_map/pallas_call | solution.py:354
  107.0 3.2 %copy.7 = f32[512,1024]{1,0:T(8,128)} copy(f32[512,1024]{1,0:T(8,128)} %shard_map.55) | data formatting | bytes 4194304
